TPU v7x, 32 devices: a whole 2x2x4 slice. The times are simulated.
32 devices in a mesh: ens: 2 (over y), lon: 4 (over z), lat: 4 (over x, core).
Axes of the slice: x: 2, y: 2, z: 4, core: 2. Of those that a mesh axis runs over, the one named last changes fastest.
Arguments:
- tracers: float32 [2, 16, 768, 512], P(None, 'ens', 'lat', 'lon'), parts along dimension 1, may hold values from -6 to 6
- velocities: float32 [2, 16, 768, 512], P(None, 'ens', 'lat', 'lon'), parts along dimension 1, may hold values from -0.6 to 0.6
- land_mask: int32 [768, 512], P('lat', 'lon'), may hold values 0 or 1
- atm_flux: float32 [768, 512], P(('ens', 'lat'), 'lon'), parts along dimension 0, may hold values from -6 to 6
- atm_id: int32 [48, 4], P('lat'), may hold values from 0 to 23, as said below
- intersection_count: int32 [48], P('lat'), may hold values from 1 to 4, as said below
- weight_tiles: float32 [48, 4, 16, 16], P('lat'), may hold values from 0 to 0.25
Outputs:
- new_tracers: float32 [2, 16, 768, 512], P(None, 'ens', 'lat', 'lon'), parts along dimension 1
- ocean_flux: float32 [1536, 512], P(('ens', 'lat'), 'lon'), parts along dimension 0
There are 2 independent parts, one for each index of `ens`. A program takes and returns all parts, laid end to end along the dimension named above; an argument that names none is the same for every part. Nothing has to cross between parts.
Inputs may be any that keep to these rules, and one draw needn't show every extreme that they name: `atm_id`: entry k of ocean block b names an atmosphere block within b // 2 - 2 to b // 2 + 2; a block's entries are consecutive blocks, the last used one repeated past its count; both ends of that reach occur. `intersection_count`: entries of a block at or past its count are ignored.
All inputs are finite; a program needn't handle non-finite values. No bound on the sum of `land_mask` on one device may be relied on, other than what follows from the above.
Results may differ from a plain program's by a relative error of at most 0.000078.
Values sent between devices are 32-bit elements; how exact they have to be, the bound alone decides.
A program may use at most 64 MiB of HBM per device.

v0:
```python
import functools

import jax
import jax.numpy as jnp
from jax import lax
from jax.experimental import pallas as pl
from jax.experimental.pallas import tpu as pltpu
from jax.sharding import PartitionSpec as P

lateral_mix = 0.06
biharmonic_mix = 0.015
vertical_mix = 0.15
heat_gain = 0.5

LANES = 128
BASE = 16
CHUNK = 16
MESH = pl.DeviceIdType.MESH
V, MASK, U = 0, 3, 4


def roll(x, shift):
    return pltpu.roll(x, shift % LANES if isinstance(shift, int) else shift, x.ndim - 1)


def kernel(
    lat_n, lon_n, levels, rows, blocks, entries, block_rows, local_atm,
    tr, vel, mask_in, atm, wt, ids, cnt, out, flux_out,
    F, G, MI, HE, HN, OE, ON, PL, A, R2, FE, FL, ATM, WT, WB,
    SNS, RNS, RC, SEW, REW,
    in_sem, out_sem, send_sem, recv_sem, atm_sem,
):
    end = BASE + rows
    tiles = rows // 8
    third = tiles // 8
    fold_rows = third * 8
    lat, lon = lax.axis_index("lat"), lax.axis_index("lon")
    top = lat == lat_n - 1
    bottom = lat == 0
    west = lax.rem(lon + lon_n - 1, lon_n)
    east = lax.rem(lon + 1, lon_n)
    up_lat = jnp.where(top, lat, lat + 1)
    up_lon = jnp.where(top, lon_n - 1 - lon, lon)
    a_lon = jnp.where(top, lax.rem(lon_n - lon, lon_n), east)
    b_lon = jnp.where(top, lax.rem(2 * lon_n - 2 - lon, lon_n), west)
    a_self = jnp.logical_and(top, a_lon == lon)
    b_self = jnp.logical_and(top, b_lon == lon)
    a_away = jnp.logical_not(a_self)
    b_away = jnp.logical_not(b_self)
    inner = jnp.logical_not(bottom)
    below = jnp.maximum(lat - 1, 0)
    up_slot = jnp.where(top, 0, 1)
    a_slot = jnp.where(top, 0, 2)
    b_slot = jnp.where(top, 1, 3)

    lane = lax.broadcasted_iota(jnp.int32, (8, LANES), 1)
    lane_c = lax.broadcasted_iota(jnp.int32, (CHUNK, LANES), 1)
    j8 = lane % 16
    jc = lane_c % 16

    loads = [
        pltpu.make_async_copy(vel.at[1], F.at[V, 0:levels, BASE:end], in_sem.at[0]),
        pltpu.make_async_copy(tr.at[0], F.at[1, 0:levels, BASE:end], in_sem.at[1]),
        pltpu.make_async_copy(tr.at[1], F.at[2, 0:levels, BASE:end], in_sem.at[2]),
        pltpu.make_async_copy(mask_in, MI, in_sem.at[3]),
        pltpu.make_async_copy(vel.at[0], F.at[U, 0:levels, BASE:end], in_sem.at[4]),
        pltpu.make_async_copy(atm, ATM.at[2 * block_rows : 2 * block_rows + local_atm * block_rows], in_sem.at[5]),
        pltpu.make_async_copy(wt, WT, in_sem.at[6]),
    ]
    for copy in (loads[5], loads[3], loads[1], loads[2], loads[4], loads[0], loads[6]):
        copy.start()

    barrier = pltpu.get_barrier_semaphore()

    def greet(lat_to, lon_to):
        pl.semaphore_signal(barrier, inc=1, device_id={"lat": lat_to, "lon": lon_to}, device_id_type=MESH)

    greet(lat, west)
    greet(lat, east)
    greet(up_lat, up_lon)
    pl.when(a_away)(lambda: greet(up_lat, a_lon))
    pl.when(b_away)(lambda: greet(up_lat, b_lon))

    @pl.when(inner)
    def _():
        greet(below, lon)
        greet(below, west)
        greet(below, east)

    zero8 = jnp.zeros((8, LANES), jnp.float32)

    def zero_slot(s, carry):
        for side in (0, 1):
            SNS[side, s, 16:24] = zero8
        return carry

    lax.fori_loop(0, 7, zero_slot, 0)

    @pl.when(bottom)
    def _():
        def clear(s, carry):
            for tile in range(3):
                RNS[1, s, 8 * tile : 8 * tile + 8] = zero8
            RC[2, s] = zero8
            RC[3, s] = zero8
            return carry

        lax.fori_loop(0, 7, clear, 0)
        for tile in range(2 * block_rows // 8):
            ATM[8 * tile : 8 * tile + 8] = zero8

    atm_end = (2 + local_atm) * block_rows

    @pl.when(top)
    def _():
        for tile in range(2 * block_rows // 8):
            ATM[atm_end + 8 * tile : atm_end + 8 * tile + 8] = zero8

    def remote(src, dst, send, recv, lat_to, lon_to):
        return pltpu.make_async_remote_copy(
            src_ref=src, dst_ref=dst, send_sem=send, recv_sem=recv,
            device_id={"lat": lat_to, "lon": lon_to}, device_id_type=MESH,
        )

    def messages(ph, n0, n1, e0, e1):
        s, r = send_sem, recv_sem
        edge = lambda side: SNS.at[side, n0:n1, 16:24]
        return {
            "up": remote(SNS.at[0, n0:n1], RNS.at[up_slot, n0:n1], s.at[ph, 0], r.at[ph, up_slot], up_lat, up_lon),
            "a": remote(edge(0), RC.at[a_slot, n0:n1], s.at[ph, 2], r.at[ph, 2 + a_slot], up_lat, a_lon),
            "b": remote(edge(0), RC.at[b_slot, n0:n1], s.at[ph, 3], r.at[ph, 2 + b_slot], up_lat, b_lon),
            "down": remote(SNS.at[1, n0:n1], RNS.at[0, n0:n1], s.at[ph, 1], r.at[ph, 0], below, lon),
            "se": remote(edge(1), RC.at[0, n0:n1], s.at[ph, 4], r.at[ph, 2], below, east),
            "sw": remote(edge(1), RC.at[1, n0:n1], s.at[ph, 5], r.at[ph, 3], below, west),
            "w": remote(SEW.at[0, e0:e1], REW.at[1, e0:e1], s.at[ph, 6], r.at[ph, 7], lat, west),
            "e": remote(SEW.at[1, e0:e1], REW.at[0, e0:e1], s.at[ph, 7], r.at[ph, 6], lat, east),
        }

    def arrivals(ph, n0, n1, e0, e1):
        s, r = send_sem, recv_sem
        edge = SNS.at[0, n0:n1, 16:24]
        got = {}
        for slot in (0, 1):
            got[slot] = remote(SNS.at[0, n0:n1], RNS.at[slot, n0:n1], s.at[ph, 0], r.at[ph, slot], lat, west)
        for slot in range(4):
            got[2 + slot] = remote(edge, RC.at[slot, n0:n1], s.at[ph, 2], r.at[ph, 2 + slot], lat, west)
        for slot in (0, 1):
            got[6 + slot] = remote(SEW.at[0, e0:e1], REW.at[slot, e0:e1], s.at[ph, 6], r.at[ph, 6 + slot], lat, west)
        return got

    def send_ew(ph, n0, n1, e0, e1):
        m = messages(ph, n0, n1, e0, e1)
        m["w"].start()
        m["e"].start()

    def send_ns(ph, n0, n1, e0, e1):
        m = messages(ph, n0, n1, e0, e1)

        @pl.when(inner)
        def _():
            m["down"].start()
            m["se"].start()
            m["sw"].start()

        @pl.when(top)
        def _():
            r_i = lax.broadcasted_iota(jnp.int32, (LANES, LANES), 0)
            c_i = lax.broadcasted_iota(jnp.int32, (LANES, LANES), 1)
            whole = jnp.where(r_i + c_i == LANES - 1, 1.0, 0.0).astype(jnp.float32)
            group = jnp.where((r_i // 16 == c_i // 16) & (r_i % 16 + c_i % 16 == 15), 1.0, 0.0).astype(jnp.float32)
            for f in range(n0, n1):
                sign = -1.0 if f == V else 1.0
                body = SNS[0, f, 0:16]
                tail = SNS[0, f, 16:24]
                SNS[0, f, 0:16] = sign * jnp.dot(
                    body, whole, precision=lax.Precision.HIGHEST, preferred_element_type=jnp.float32
                )
                SNS[0, f, 16:24] = sign * jnp.dot(
                    tail, group, precision=lax.Precision.HIGHEST, preferred_element_type=jnp.float32
                )

        m["up"].start()
        pl.when(a_away)(m["a"].start)
        pl.when(b_away)(m["b"].start)

        @pl.when(a_self)
        def _():
            for f in range(n0, n1):
                RC[0, f] = SNS[0, f, 16:24]

        @pl.when(b_self)
        def _():
            for f in range(n0, n1):
                RC[1, f] = SNS[0, f, 16:24]

    def wait_all(ph, n0, n1, e0, e1):
        got = arrivals(ph, n0, n1, e0, e1)
        got[0].wait_recv()
        pl.when(a_away)(got[2].wait_recv)
        pl.when(b_away)(got[3].wait_recv)
        got[6].wait_recv()
        got[7].wait_recv()

        @pl.when(inner)
        def _():
            got[1].wait_recv()
            got[4].wait_recv()
            got[5].wait_recv()

    def wait_sent(ph, n0, n1, e0, e1):
        m = messages(ph, n0, n1, e0, e1)
        m["up"].wait_send()
        m["w"].wait_send()
        m["e"].wait_send()
        pl.when(a_away)(m["a"].wait_send)
        pl.when(b_away)(m["b"].wait_send)

        @pl.when(inner)
        def _():
            m["down"].wait_send()
            m["se"].wait_send()
            m["sw"].wait_send()

    def finish_pack(B, s, gather):
        to_w = [zero8] * third
        to_e = [zero8] * third
        for i in range(tiles):
            a = gather(i)
            own = jnp.where(j8 < 8, roll(a, -4), roll(a, 4))
            B[levels, BASE + 8 * i : BASE + 8 * i + 8] = own
            p, r = i // third, i % third
            here = j8 // 2 == p
            to_w[r] = jnp.where(here, roll(own, 2 * p - 4), to_w[r])
            to_e[r] = jnp.where(here, roll(own, 2 * p - 10), to_e[r])
        for r in range(third):
            SEW[0, s, 8 * r : 8 * r + 8] = to_w[r]
            SEW[1, s, 8 * r : 8 * r + 8] = to_e[r]

    def pack_rows(B, s):
        for side, first, second in ((0, end - 1, end - 2), (1, BASE, BASE + 1)):
            for l in range(levels):
                SNS[side, s, l : l + 1] = B[l, first : first + 1]
                SNS[side, s, levels + l : levels + l + 1] = B[l, second : second + 1]
            SNS[side, s, 16:17] = B[levels, first : first + 1]
            SNS[side, s, 17:18] = B[levels, second : second + 1]

    def gather_planes(B):
        def gather(i):
            a = zero8
            for l in range(levels):
                a = jnp.where(lane // 16 == l, roll(B[l, BASE + 8 * i : BASE + 8 * i + 8], 16 * l + 8), a)
            return a

        return gather

    def unpack_rows(B, s):
        for l in range(levels):
            B[l, end : end + 1] = RNS[0, s, l : l + 1]
            B[l, end + 1 : end + 2] = RNS[0, s, levels + l : levels + l + 1]
            B[l, BASE - 1 : BASE] = RNS[1, s, l : l + 1]
            B[l, BASE - 2 : BASE - 1] = RNS[1, s, levels + l : levels + l + 1]
        for side, first, second in ((0, end, end + 1), (1, BASE - 1, BASE - 2)):
            own = RNS[side, s, 16:24]
            w = roll(RC[2 * side, s], -8)
            e = roll(RC[2 * side + 1, s], 8)
            x = jnp.where(j8 < 4, w, jnp.where(j8 >= 12, e, own))
            B[levels, first : first + 1] = x[0:1]
            B[levels, second : second + 1] = x[1:2]

    def unpack_cols(B, s):
        for i in range(tiles):
            p, r = i // third, i % third
            at = slice(BASE + 8 * i, BASE + 8 * i + 8)
            w = roll(REW[0, s, 8 * r : 8 * r + 8], 2 - 2 * p)
            e = roll(REW[1, s, 8 * r : 8 * r + 8], 12 - 2 * p)
            B[levels, at] = jnp.where(j8 < 4, w, jnp.where(j8 >= 12, e, B[levels, at]))

    pl.semaphore_wait(
        barrier, 3 + jnp.where(a_away, 1, 0) + jnp.where(b_away, 1, 0) + jnp.where(inner, 3, 0)
    )
    reach = 2 * block_rows
    loads[5].wait()
    atm_up = remote(ATM.at[atm_end - reach : atm_end], ATM.at[0:reach], atm_sem.at[0], atm_sem.at[2], up_lat, up_lon)
    atm_down = remote(
        ATM.at[reach : 2 * reach], ATM.at[atm_end : atm_end + reach], atm_sem.at[1], atm_sem.at[3], below, lon
    )
    pl.when(jnp.logical_not(top))(atm_up.start)
    pl.when(inner)(atm_down.start)

    loads[3].wait()

    def spread_mask(l, carry):
        F[MASK, l, BASE:end] = MI[...].astype(jnp.float32)
        return carry

    lax.fori_loop(0, levels, spread_mask, 0)
    for index in (1, 2, 4, 0):
        loads[index].wait()

    def pack_field(f, carry):
        B = F.at[f]
        finish_pack(B, f, gather_planes(B))
        pack_rows(B, f)
        return carry

    lax.fori_loop(0, 5, pack_field, 0)
    first = (0, 0, 4, 1, 5)
    send_ew(*first)
    send_ns(*first)

    loads[6].wait()
    slots = local_atm + 4
    wide = slots * block_rows
    spread = jnp.where(
        lax.broadcasted_iota(jnp.int32, (block_rows, wide), 1) % block_rows
        == lax.broadcasted_iota(jnp.int32, (block_rows, wide), 0),
        1.0, 0.0,
    ).astype(jnp.float32)
    slot_of = lax.broadcasted_iota(jnp.int32, (block_rows, wide), 1) // block_rows

    def build(b, carry):
        flat = jnp.concatenate([WT[b, k] for k in range(entries)], 0)
        copies = jnp.dot(flat, spread, precision=lax.Precision.HIGHEST, preferred_element_type=jnp.float32)
        total = jnp.zeros((block_rows, wide), jnp.float32)
        for k in range(entries):
            slot = jnp.where(k < cnt[b], ids[b, k] - lat * local_atm + 2, -1)
            total = total + jnp.where(slot_of == slot, copies[k * block_rows : (k + 1) * block_rows], 0.0)
        WB[pl.ds(pl.multiple_of(b * block_rows, block_rows), block_rows)] = total
        return carry

    lax.fori_loop(0, blocks, build, 0)
    pl.when(inner)(
        remote(ATM.at[0:reach], ATM.at[0:reach], atm_sem.at[0], atm_sem.at[2], lat, west).wait_recv
    )
    pl.when(jnp.logical_not(top))(
        remote(ATM.at[0:reach], ATM.at[atm_end : atm_end + reach], atm_sem.at[1], atm_sem.at[3], lat, west).wait_recv
    )
    FL[...] = jnp.dot(WB[...], ATM[...], precision=lax.Precision.HIGHEST, preferred_element_type=jnp.float32)
    flux_copy = pltpu.make_async_copy(FL, flux_out, in_sem.at[7])
    flux_copy.start()
    for i in range(tiles):
        at = slice(8 * i, 8 * i + 8)
        a = roll(FL[at], 8)
        own = jnp.where(j8 < 8, roll(a, -4), roll(a, 4))
        FE[at] = jnp.where(lane < 16, heat_gain * own, 0.0)

    wait_all(*first)

    def place_rows(f, carry):
        unpack_rows(F.at[f], f)
        return carry

    def place_cols(f, carry):
        unpack_cols(F.at[f], f)
        return carry

    lax.fori_loop(0, 4, place_rows, 0)
    lax.fori_loop(1, 5, place_cols, 0)

    for kind, plane in ((0, 0), (1, levels)):
        for r in range(8, end + 8, 8):
            m = F[MASK, plane, r : r + 8]
            OE[kind, r : r + 8] = m * roll(m, -1)
            ON[kind, r : r + 8] = m * F[MASK, plane, r + 1 : r + 9]

    def face_tables(l, carry):
        kind = jnp.where(l == levels, 1, 0)
        for r in range(8, end, 8):
            at = slice(r, r + 8)
            HN[l, at] = 0.25 * ON[kind, at] * (F[V, l, at] + F[V, l, r + 1 : r + 9])
            if r >= BASE:
                u = F[U, l, at]
                HE[l, at] = 0.25 * OE[kind, at] * (u + roll(u, -1))
        return carry

    lax.fori_loop(0, levels + 1, face_tables, 0)

    def first_pass(B, l, kind):
        for r in range(8, end + 8, CHUNK):
            at = slice(r, r + CHUNK)
            q = B[l, at]
            ge = OE[kind, at] * (roll(q, -1) - q)
            lap = (ge - roll(ge, 1)) + (
                ON[kind, at] * (B[l, r + 1 : r + 1 + CHUNK] - q)
                - ON[kind, r - 1 : r - 1 + CHUNK] * (q - B[l, r - 1 : r - 1 + CHUNK])
            )
            PL[at] = biharmonic_mix * lap - lateral_mix * q

    def second_pass(B, l, kind, r, vertical, heat):
        at, up, dn = slice(r, r + CHUNK), slice(r + 1, r + 1 + CHUNK), slice(r - 1, r - 1 + CHUNK)
        q, qn, qs = B[l, at], B[l, up], B[l, dn]
        p, pn, ps = PL[at], PL[up], PL[dn]
        te = HE[l, at] * (q + roll(q, -1)) + OE[kind, at] * (roll(p, -1) - p)
        tn = HN[l, at] * (q + qn) + ON[kind, at] * (pn - p)
        ts = HN[l, dn] * (q + qs) + ON[kind, dn] * (p - ps)
        low, high = vertical(q, at)
        change = vertical_mix * ((low - q) + (high - q)) - ((te - roll(te, 1)) + (tn - ts))
        if heat is not None:
            change = change + heat
        return q + F[MASK, levels if kind == 1 else 0, at] * change

    def advance(B, C, t, packing):
        first_pass(B, levels, 1)
        for r in range(BASE, end, CHUNK):
            own = slice(r - BASE, r - BASE + CHUNK)

            def beside(q, at):
                return (
                    jnp.where(lane_c < 16, q, roll(q, 16)),
                    jnp.where(lane_c >= LANES - 16, q, roll(q, -16)),
                )

            res = second_pass(B, levels, 1, r, beside, FE[own] if t == 0 else None)
            R2[own] = jnp.where(jc < 2, roll(res, -10), roll(res, -2))

        def level(l, carry):
            first_pass(B, l, 0)
            back = lax.rem(2 * LANES - 2 - 16 * l, LANES)
            ahead = lax.rem(16 * l + 8, LANES)
            lower, upper = jnp.maximum(l - 1, 0), jnp.minimum(l + 1, levels - 1)
            gain = jnp.where(l == 0, heat_gain, 0.0).astype(jnp.float32)
            for r in range(BASE, end, CHUNK):
                own = slice(r - BASE, r - BASE + CHUNK)
                res = second_pass(
                    B, l, 0, r, lambda q, at: (B[lower, at], B[upper, at]), gain * FL[own] if t == 0 else None
                )
                res = jnp.where((lane_c < 2) | (lane_c >= LANES - 2), roll(R2[own], back), res)
                C[l, r : r + CHUNK] = res
                if packing:
                    A[own] = jnp.where(lane_c // 16 == l, roll(res, ahead), A[own])
            if not packing:
                pltpu.make_async_copy(C.at[l, BASE:end], out.at[t, l], out_sem.at[t, l]).start()
            return carry

        lax.fori_loop(0, levels, level, 0)

    later = ((1, 5, 6, 5, 6), (2, 6, 7, 6, 7))
    for t in (0, 1):
        advance(F.at[1 + t], G.at[t], t, True)
        finish_pack(G.at[t], 5 + t, lambda i: A[8 * i : 8 * i + 8])
        send_ew(*later[t])
        pack_rows(G.at[t], 5 + t)
        send_ns(*later[t])
    for t in (0, 1):
        wait_all(*later[t])
        unpack_rows(G.at[t], 5 + t)
        unpack_cols(G.at[t], 5 + t)
        advance(G.at[t], F.at[1 + t], t, False)

    pl.when(jnp.logical_not(top))(atm_up.wait_send)
    pl.when(inner)(atm_down.wait_send)
    wait_sent(*first)
    for t in (0, 1):
        wait_sent(*later[t])
    flux_copy.wait()

    def finish(l, carry):
        for t in (0, 1):
            pltpu.make_async_copy(F.at[1 + t, l, BASE:end], out.at[t, l], out_sem.at[t, l]).wait()
        return carry

    lax.fori_loop(0, levels, finish, 0)


def solution(mesh):
    lat_n, lon_n = mesh.shape["lat"], mesh.shape["lon"]

    def per_device(tracers, velocities, land_mask, atm_flux, atm_id, intersection_count, weight_tiles):
        _, levels, rows, cols = tracers.shape
        blocks, entries, block_rows, _ = weight_tiles.shape
        local_atm = atm_flux.shape[0] // block_rows
        planes = levels + 1
        tall = rows + 2 * BASE
        fold_rows = rows // 8
        f32 = jnp.float32
        hbm = pl.BlockSpec(memory_space=pl.ANY)
        smem = pl.BlockSpec(memory_space=pltpu.SMEM)
        return pl.pallas_call(
            functools.partial(kernel, lat_n, lon_n, levels, rows, blocks, entries, block_rows, local_atm),
            out_shape=(
                jax.ShapeDtypeStruct(tracers.shape, f32),
                jax.ShapeDtypeStruct((rows, cols), f32),
            ),
            in_specs=[hbm, hbm, hbm, hbm, hbm, smem, smem],
            out_specs=(hbm, hbm),
            scratch_shapes=[
                pltpu.VMEM((5, planes, tall, cols), f32),
                pltpu.VMEM((2, planes, tall, cols), f32),
                pltpu.VMEM((rows, cols), jnp.int32),
                pltpu.VMEM((planes, tall, cols), f32),
                pltpu.VMEM((planes, tall, cols), f32),
                pltpu.VMEM((2, tall, cols), f32),
                pltpu.VMEM((2, tall, cols), f32),
                pltpu.VMEM((tall, cols), f32),
                pltpu.VMEM((rows, cols), f32),
                pltpu.VMEM((rows, cols), f32),
                pltpu.VMEM((rows, cols), f32),
                pltpu.VMEM((rows, cols), f32),
                pltpu.VMEM(((local_atm + 4) * block_rows, cols), f32),
                pltpu.VMEM(weight_tiles.shape, f32),
                pltpu.VMEM((rows, (local_atm + 4) * block_rows), f32),
                pltpu.VMEM((2, 7, 24, cols), f32),
                pltpu.VMEM((2, 7, 24, cols), f32),
                pltpu.VMEM((4, 7, 8, cols), f32),
                pltpu.VMEM((2, 7, fold_rows, cols), f32),
                pltpu.VMEM((2, 7, fold_rows, cols), f32),
                pltpu.SemaphoreType.DMA((8,)),
                pltpu.SemaphoreType.DMA((2, levels)),
                pltpu.SemaphoreType.DMA((3, 8)),
                pltpu.SemaphoreType.DMA((3, 8)),
                pltpu.SemaphoreType.DMA((4,)),
            ],
            compiler_params=pltpu.CompilerParams(
                collective_id=0, has_side_effects=True, vmem_limit_bytes=40 * 1024 * 1024
            ),
        )(tracers, velocities, land_mask, atm_flux, weight_tiles, atm_id, intersection_count)

    in_specs = (
        P(None, "ens", "lat", "lon"),
        P(None, "ens", "lat", "lon"),
        P("lat", "lon"),
        P(("ens", "lat"), "lon"),
        P("lat", None),
        P("lat"),
        P("lat", None, None, None),
    )
    out_specs = (P(None, "ens", "lat", "lon"), P(("ens", "lat"), "lon"))
    return jax.shard_map(
        per_device, mesh=mesh, in_specs=in_specs, out_specs=out_specs, check_vma=False
    )
```

profile of v0, /device:TPU:1, one launch (start us, length us, event | category | flops | bytes accessed | tf_op | source)
XLA Modules:
  0.0 49.1 jit_solution(9428939824085386772)
XLA Ops:
  0.6 0.8 %copy.9.ids = s32[12,4]{1,0:T(8,128)S(1)} copy(s32[12,4]{0,1:T(4,128)} %param.11) | data formatting | bytes 384 | tf_op args[4]
  1.4 0.0 copy-start
  1.4 1.4 %copy-done = f32[2,8,192,128]{3,2,1,0:T(8,128)S(1)} copy-done((f32[2,8,192,128]{3,2,1,0:T(8,128)S(1)}, f32[2,8,192,128]{3,2,1,0:T(8,128)}, u32[]{:S(2)}) %copy-start) | copy-done | bytes 1572888
  2.8 0.0 copy-start.1
  2.8 1.4 %copy-done.1 = f32[2,8,192,128]{3,2,1,0:T(8,128)S(1)} copy-done((f32[2,8,192,128]{3,2,1,0:T(8,128)S(1)}, f32[2,8,192,128]{3,2,1,0:T(8,128)}, u32[]{:S(2)}) %copy-start.1) | copy-done | bytes 1572888
  4.2 0.0 copy-start.2
  4.2 1.0 %copy-done.2 = f32[12,4,16,16]{3,2,1,0:T(8,128)S(1)} copy-done((f32[12,4,16,16]{3,2,1,0:T(8,128)S(1)}, f32[12,4,16,16]{3,2,1,0:T(8,128)}, u32[]{:S(2)}) %copy-start.2) | copy-done | bytes 49176
  5.2 0.0 copy-start.3
  5.2 0.9 %copy-done.3 = s32[192,128]{1,0:T(8,128)S(1)} copy-done((s32[192,128]{1,0:T(8,128)S(1)}, s32[192,128]{1,0:T(8,128)}, u32[]{:S(2)}) %copy-start.3) | copy-done | bytes 98328
  6.1 0.0 copy-start.4
  6.1 0.8 %copy-done.4 = f32[96,128]{1,0:T(8,128)S(1)} copy-done((f32[96,128]{1,0:T(8,128)S(1)}, f32[96,128]{1,0:T(8,128)}, u32[]{:S(2)}) %copy-start.4) | copy-done | bytes 49176
  6.9 0.0 copy-start.5
  6.9 0.7 %copy-done.5 = s32[12]{0:T(128)S(1)} copy-done((s32[12]{0:T(128)S(1)}, s32[12]{0:T(128)}, u32[]{:S(2)}) %copy-start.5) | copy-done | bytes 72
  7.6 39.8 %shard_map.86 = (f32[2,8,192,128]{3,2,1,0:T(8,128)S(1)}, f32[192,128]{1,0:T(8,128)S(1)}) custom-call(f32[2,8,192,128]{3,2,1,0:T(8,128)S(1)} %copy-done, f32[2,8,192,128]{3,2,1,0:T(8,128)S(1)} %copy-done.1, s32[192,128]{1,0:T(8,128)S(1)} %copy-done.3, f32[96,128]{1,0:T(8,128)S(1)} %copy-done.4, f32[12,4,16,16]{3,2,1,0:T(8,128)S(1)} %copy-done.2, ...), custom_call_target="tpu_custom_call" | custom-call | tf_op jit(solution)/shard_map/pallas_call | solution.py:478
  47.4 1.1 %copy.12 = f32[2,8,192,128]{3,2,1,0:T(8,128)} copy(f32[2,8,192,128]{3,2,1,0:T(8,128)S(1)} %get-tuple-element.4) | data formatting | bytes 3145728
  48.5 0.6 %copy.13 = f32[192,128]{1,0:T(8,128)} copy(f32[192,128]{1,0:T(8,128)S(1)} %get-tuple-element.5) | data formatting | bytes 196608
Async XLA Ops:
  1.4 1.4 %copy-start = (f32[2,8,192,128]{3,2,1,0:T(8,128)S(1)}, f32[2,8,192,128]{3,2,1,0:T(8,128)}, u32[]{:S(2)}) copy-start(f32[2,8,192,128]{3,2,1,0:T(8,128)} %tr.1) | copy-start | bytes 4718596
  2.8 1.4 %copy-start.1 = (f32[2,8,192,128]{3,2,1,0:T(8,128)S(1)}, f32[2,8,192,128]{3,2,1,0:T(8,128)}, u32[]{:S(2)}) copy-start(f32[2,8,192,128]{3,2,1,0:T(8,128)} %vel.1) | copy-start | bytes 4718596
  4.2 1.0 %copy-start.2 = (f32[12,4,16,16]{3,2,1,0:T(8,128)S(1)}, f32[12,4,16,16]{3,2,1,0:T(8,128)}, u32[]{:S(2)}) copy-start(f32[12,4,16,16]{3,2,1,0:T(8,128)} %wt.1) | copy-start | bytes 147460
  5.2 0.9 %copy-start.3 = (s32[192,128]{1,0:T(8,128)S(1)}, s32[192,128]{1,0:T(8,128)}, u32[]{:S(2)}) copy-start(s32[192,128]{1,0:T(8,128)} %mask_in.1) | copy-start | bytes 294916
  6.1 0.8 %copy-start.4 = (f32[96,128]{1,0:T(8,128)S(1)}, f32[96,128]{1,0:T(8,128)}, u32[]{:S(2)}) copy-start(f32[96,128]{1,0:T(8,128)} %atm.1) | copy-start | bytes 147460
  6.9 0.7 %copy-start.5 = (s32[12]{0:T(128)S(1)}, s32[12]{0:T(128)}, u32[]{:S(2)}) copy-start(s32[12]{0:T(128)} %cnt.1) | copy-start | bytes 148
where the time goes:
time: 49.5 us; the launch traced here: 49.1 us
  Pallas kernels  39.8 us (80%)
  local copies, waits for them, and re-layouts  8.71 us (18%)
  between operations  0.64 us (1%)
    pallas_call x1, Pallas kernels, per_device(): pl.pallas_call(functools.partial(kernel, lat_n, lon_n, levels, rows, bloc...  39.8 us
    unnamed x15, local copies, waits for them, and re-layouts  8.71 us

commit v1 on v0

--- a/solution.py
+++ b/solution.py
@@ -55,8 +55,14 @@
 
     lane = lax.broadcasted_iota(jnp.int32, (8, LANES), 1)
     lane_c = lax.broadcasted_iota(jnp.int32, (CHUNK, LANES), 1)
-    j8 = lane % 16
-    jc = lane_c % 16
+    j8 = lane & 15
+    group8 = lane >> 4
+    pair8 = j8 >> 1
+    low8, high8, half8 = j8 < 4, j8 >= 12, j8 < 8
+    group_c = lane_c >> 4
+    jc_low = (lane_c & 15) < 2
+    rim_c = (lane_c < 2) | (lane_c >= LANES - 2)
+    first_c, last_c = lane_c < 16, lane_c >= LANES - 16
 
     loads = [
         pltpu.make_async_copy(vel.at[1], F.at[V, 0:levels, BASE:end], in_sem.at[0]),
@@ -168,16 +174,15 @@
             c_i = lax.broadcasted_iota(jnp.int32, (LANES, LANES), 1)
             whole = jnp.where(r_i + c_i == LANES - 1, 1.0, 0.0).astype(jnp.float32)
             group = jnp.where((r_i // 16 == c_i // 16) & (r_i % 16 + c_i % 16 == 15), 1.0, 0.0).astype(jnp.float32)
-            for f in range(n0, n1):
-                sign = -1.0 if f == V else 1.0
-                body = SNS[0, f, 0:16]
-                tail = SNS[0, f, 16:24]
-                SNS[0, f, 0:16] = sign * jnp.dot(
-                    body, whole, precision=lax.Precision.HIGHEST, preferred_element_type=jnp.float32
-                )
-                SNS[0, f, 16:24] = sign * jnp.dot(
-                    tail, group, precision=lax.Precision.HIGHEST, preferred_element_type=jnp.float32
-                )
+            count = n1 - n0
+            body = jnp.concatenate([SNS[0, f, 0:16] for f in range(n0, n1)], 0)
+            tail = jnp.concatenate([SNS[0, f, 16:24] for f in range(n0, n1)], 0)
+            body = jnp.dot(body, whole, precision=lax.Precision.HIGHEST, preferred_element_type=jnp.float32)
+            tail = jnp.dot(tail, group, precision=lax.Precision.HIGHEST, preferred_element_type=jnp.float32)
+            for i in range(count):
+                sign = -1.0 if n0 + i == V else 1.0
+                SNS[0, n0 + i, 0:16] = sign * body[16 * i : 16 * i + 16]
+                SNS[0, n0 + i, 16:24] = sign * tail[8 * i : 8 * i + 8]
 
         m["up"].start()
         pl.when(a_away)(m["a"].start)
@@ -224,12 +229,12 @@
     def finish_pack(B, s, gather):
         to_w = [zero8] * third
         to_e = [zero8] * third
-        for i in range(tiles):
-            a = gather(i)
-            own = jnp.where(j8 < 8, roll(a, -4), roll(a, 4))
+        gathered = [gather(i) for i in range(tiles)]
+        owns = [jnp.where(half8, roll(a, -4), roll(a, 4)) for a in gathered]
+        for i, own in enumerate(owns):
             B[levels, BASE + 8 * i : BASE + 8 * i + 8] = own
             p, r = i // third, i % third
-            here = j8 // 2 == p
+            here = pair8 == p
             to_w[r] = jnp.where(here, roll(own, 2 * p - 4), to_w[r])
             to_e[r] = jnp.where(here, roll(own, 2 * p - 10), to_e[r])
         for r in range(third):
@@ -248,7 +253,7 @@
         def gather(i):
             a = zero8
             for l in range(levels):
-                a = jnp.where(lane // 16 == l, roll(B[l, BASE + 8 * i : BASE + 8 * i + 8], 16 * l + 8), a)
+                a = jnp.where(group8 == l, roll(B[l, BASE + 8 * i : BASE + 8 * i + 8], 16 * l + 8), a)
             return a
 
         return gather
@@ -263,7 +268,7 @@
             own = RNS[side, s, 16:24]
             w = roll(RC[2 * side, s], -8)
             e = roll(RC[2 * side + 1, s], 8)
-            x = jnp.where(j8 < 4, w, jnp.where(j8 >= 12, e, own))
+            x = jnp.where(low8, w, jnp.where(high8, e, own))
             B[levels, first : first + 1] = x[0:1]
             B[levels, second : second + 1] = x[1:2]
 
@@ -273,7 +278,25 @@
             at = slice(BASE + 8 * i, BASE + 8 * i + 8)
             w = roll(REW[0, s, 8 * r : 8 * r + 8], 2 - 2 * p)
             e = roll(REW[1, s, 8 * r : 8 * r + 8], 12 - 2 * p)
-            B[levels, at] = jnp.where(j8 < 4, w, jnp.where(j8 >= 12, e, B[levels, at]))
+            B[levels, at] = jnp.where(low8, w, jnp.where(high8, e, B[levels, at]))
+
+    loads[3].wait()
+
+    def spread_mask(l, carry):
+        F[MASK, l, BASE:end] = MI[...].astype(jnp.float32)
+        return carry
+
+    lax.fori_loop(0, levels, spread_mask, 0)
+    def pack_field(f, carry):
+        B = F.at[f]
+        finish_pack(B, f, gather_planes(B))
+        pack_rows(B, f)
+        return carry
+
+    for f in (MASK, 1, 2, U, V):
+        if f != MASK:
+            loads[f].wait()
+        pack_field(f, 0)
 
     pl.semaphore_wait(
         barrier, 3 + jnp.where(a_away, 1, 0) + jnp.where(b_away, 1, 0) + jnp.where(inner, 3, 0)
@@ -287,23 +310,6 @@
     pl.when(jnp.logical_not(top))(atm_up.start)
     pl.when(inner)(atm_down.start)
 
-    loads[3].wait()
-
-    def spread_mask(l, carry):
-        F[MASK, l, BASE:end] = MI[...].astype(jnp.float32)
-        return carry
-
-    lax.fori_loop(0, levels, spread_mask, 0)
-    for index in (1, 2, 4, 0):
-        loads[index].wait()
-
-    def pack_field(f, carry):
-        B = F.at[f]
-        finish_pack(B, f, gather_planes(B))
-        pack_rows(B, f)
-        return carry
-
-    lax.fori_loop(0, 5, pack_field, 0)
     first = (0, 0, 4, 1, 5)
     send_ew(*first)
     send_ns(*first)
@@ -323,7 +329,7 @@
         copies = jnp.dot(flat, spread, precision=lax.Precision.HIGHEST, preferred_element_type=jnp.float32)
         total = jnp.zeros((block_rows, wide), jnp.float32)
         for k in range(entries):
-            slot = jnp.where(k < cnt[b], ids[b, k] - lat * local_atm + 2, -1)
+            slot = jnp.where(k < cnt[b], ids[k, b] - lat * local_atm + 2, -1)
             total = total + jnp.where(slot_of == slot, copies[k * block_rows : (k + 1) * block_rows], 0.0)
         WB[pl.ds(pl.multiple_of(b * block_rows, block_rows), block_rows)] = total
         return carry
@@ -341,7 +347,7 @@
     for i in range(tiles):
         at = slice(8 * i, 8 * i + 8)
         a = roll(FL[at], 8)
-        own = jnp.where(j8 < 8, roll(a, -4), roll(a, 4))
+        own = jnp.where(half8, roll(a, -4), roll(a, 4))
         FE[at] = jnp.where(lane < 16, heat_gain * own, 0.0)
 
     wait_all(*first)
@@ -406,12 +412,12 @@
 
             def beside(q, at):
                 return (
-                    jnp.where(lane_c < 16, q, roll(q, 16)),
-                    jnp.where(lane_c >= LANES - 16, q, roll(q, -16)),
+                    jnp.where(first_c, q, roll(q, 16)),
+                    jnp.where(last_c, q, roll(q, -16)),
                 )
 
             res = second_pass(B, levels, 1, r, beside, FE[own] if t == 0 else None)
-            R2[own] = jnp.where(jc < 2, roll(res, -10), roll(res, -2))
+            R2[own] = jnp.where(jc_low, roll(res, -10), roll(res, -2))
 
         def level(l, carry):
             first_pass(B, l, 0)
@@ -424,10 +430,10 @@
                 res = second_pass(
                     B, l, 0, r, lambda q, at: (B[lower, at], B[upper, at]), gain * FL[own] if t == 0 else None
                 )
-                res = jnp.where((lane_c < 2) | (lane_c >= LANES - 2), roll(R2[own], back), res)
+                res = jnp.where(rim_c, roll(R2[own], back), res)
                 C[l, r : r + CHUNK] = res
                 if packing:
-                    A[own] = jnp.where(lane_c // 16 == l, roll(res, ahead), A[own])
+                    A[own] = jnp.where(group_c == l, roll(res, ahead), A[own])
             if not packing:
                 pltpu.make_async_copy(C.at[l, BASE:end], out.at[t, l], out_sem.at[t, l]).start()
             return carry
@@ -473,7 +479,7 @@
         tall = rows + 2 * BASE
         fold_rows = rows // 8
         f32 = jnp.float32
-        hbm = pl.BlockSpec(memory_space=pl.ANY)
+        hbm = pl.BlockSpec(memory_space=pltpu.HBM)
         smem = pl.BlockSpec(memory_space=pltpu.SMEM)
         return pl.pallas_call(
             functools.partial(kernel, lat_n, lon_n, levels, rows, blocks, entries, block_rows, local_atm),
@@ -511,9 +517,9 @@
                 pltpu.SemaphoreType.DMA((4,)),
             ],
             compiler_params=pltpu.CompilerParams(
-                collective_id=0, has_side_effects=True, vmem_limit_bytes=40 * 1024 * 1024
+                collective_id=0, has_side_effects=True, vmem_limit_bytes=62 * 1024 * 1024
             ),
-        )(tracers, velocities, land_mask, atm_flux, weight_tiles, atm_id, intersection_count)
+        )(tracers, velocities, land_mask, atm_flux, weight_tiles, atm_id.T, intersection_count)
 
     in_specs = (
         P(None, "ens", "lat", "lon"),

time: 49.5 us -> 35.8 us (0.72)
  Pallas kernels: 39.8 us -> 31.6 us
  local copies, waits for them, and re-layouts: 8.71 us -> 3.38 us
    pallas_call x1, Pallas kernels: 39.8 us -> 31.6 us  [per_device(): pl.pallas_call(functools.partial(kernel, lat_n, lon_n, levels, rows, bloc...]
    unnamed x15 -> x4, local copies, waits for them, and re-layouts: 8.71 us -> 3.38 us
where the time goes in v1:
time: 35.8 us; the launch traced here: 35.6 us
  Pallas kernels  31.6 us (88%)
  local copies, waits for them, and re-layouts  3.38 us (9%)
  between operations  0.65 us (2%)
    pallas_call x1, Pallas kernels, per_device(): pl.pallas_call(functools.partial(kernel, lat_n, lon_n, levels, rows, bloc...  31.6 us
    unnamed x4, local copies, waits for them, and re-layouts  3.38 us

profile of v1, /device:TPU:1, one launch (start us, length us, event | category | flops | bytes accessed | tf_op | source)
XLA Modules:
  0.0 35.6 jit_solution(12450129238753347951)
XLA Ops:
  0.6 31.6 %shard_map.86 = (f32[2,8,192,128]{3,2,1,0:T(8,128)}, f32[192,128]{1,0:T(8,128)}) custom-call(f32[2,8,192,128]{3,2,1,0:T(8,128)} %tr.1, f32[2,8,192,128]{3,2,1,0:T(8,128)} %vel.1, s32[192,128]{1,0:T(8,128)} %mask_in.1, f32[96,128]{1,0:T(8,128)} %atm.1, f32[12,4,16,16]{3,2,1,0:T(8,128)} %wt.1, s32[4,12]{1,0:T(4,128)} %bitcast.1, s32[12]{0:T(128)} %cnt.1), custom_call_target="tpu_custom_call" | custom-call | tf_op jit(solution)/shard_map/pallas_call | solution.py:484
  32.2 0.0 copy-start
  32.2 2.7 %copy.11 = f32[2,8,192,128]{3,2,1,0:T(8,128)} copy(f32[2,8,192,128]{3,2,1,0:T(8,128)} %get-tuple-element.4) | data formatting | bytes 3145728
  34.9 0.0 copy-done
  34.9 0.6 %copy.12 = f32[192,128]{1,0:T(8,128)} copy(f32[192,128]{1,0:T(8,128)S(1)} %copy-done) | data formatting | bytes 196608
Async XLA Ops:
  32.2 2.7 %copy-start = (f32[192,128]{1,0:T(8,128)S(1)}, f32[192,128]{1,0:T(8,128)}, u32[]{:S(2)}) copy-start(f32[192,128]{1,0:T(8,128)} %get-tuple-element.5) | copy-start | bytes 294916

commit v2 on v1

--- a/solution.py
+++ b/solution.py
@@ -14,7 +14,7 @@
 
 LANES = 128
 BASE = 16
-CHUNK = 16
+CHUNK = 32
 MESH = pl.DeviceIdType.MESH
 V, MASK, U = 0, 3, 4
 
@@ -350,45 +350,59 @@
         own = jnp.where(half8, roll(a, -4), roll(a, 4))
         FE[at] = jnp.where(lane < 16, heat_gain * own, 0.0)
 
-    wait_all(*first)
-
-    def place_rows(f, carry):
-        unpack_rows(F.at[f], f)
-        return carry
-
-    def place_cols(f, carry):
-        unpack_cols(F.at[f], f)
-        return carry
-
-    lax.fori_loop(0, 4, place_rows, 0)
-    lax.fori_loop(1, 5, place_cols, 0)
-
-    for kind, plane in ((0, 0), (1, levels)):
-        for r in range(8, end + 8, 8):
+    def mask_tables(kind, plane, starts):
+        for r in starts:
             m = F[MASK, plane, r : r + 8]
             OE[kind, r : r + 8] = m * roll(m, -1)
             ON[kind, r : r + 8] = m * F[MASK, plane, r + 1 : r + 9]
 
-    def face_tables(l, carry):
-        kind = jnp.where(l == levels, 1, 0)
-        for r in range(8, end, 8):
+    def face_tables(l, kind, starts):
+        for r in starts:
             at = slice(r, r + 8)
             HN[l, at] = 0.25 * ON[kind, at] * (F[V, l, at] + F[V, l, r + 1 : r + 9])
             if r >= BASE:
                 u = F[U, l, at]
                 HE[l, at] = 0.25 * OE[kind, at] * (u + roll(u, -1))
-        return carry
-
-    lax.fori_loop(0, levels + 1, face_tables, 0)
+
+    mask_tables(0, 0, range(BASE, end - 8, 8))
+
+    def own_tables(l, carry):
+        face_tables(l, 0, range(BASE, end - 8, 8))
+        return carry
+
+    lax.fori_loop(0, levels, own_tables, 0)
+
+    wait_all(*first)
+
+    def place_rows(f, carry):
+        unpack_rows(F.at[f], f)
+        return carry
+
+    def place_cols(f, carry):
+        unpack_cols(F.at[f], f)
+        return carry
+
+    lax.fori_loop(0, 4, place_rows, 0)
+    lax.fori_loop(1, 5, place_cols, 0)
+
+    mask_tables(0, 0, (8, end - 8, end))
+    mask_tables(1, levels, range(8, end + 8, 8))
+
+    def rim_tables(l, carry):
+        face_tables(l, 0, (8, end - 8))
+        return carry
+
+    lax.fori_loop(0, levels, rim_tables, 0)
+    face_tables(levels, 1, range(8, end, 8))
 
     def first_pass(B, l, kind):
-        for r in range(8, end + 8, CHUNK):
-            at = slice(r, r + CHUNK)
+        for r in range(8, end + 8, 16):
+            at = slice(r, r + 16)
             q = B[l, at]
             ge = OE[kind, at] * (roll(q, -1) - q)
             lap = (ge - roll(ge, 1)) + (
-                ON[kind, at] * (B[l, r + 1 : r + 1 + CHUNK] - q)
-                - ON[kind, r - 1 : r - 1 + CHUNK] * (q - B[l, r - 1 : r - 1 + CHUNK])
+                ON[kind, at] * (B[l, r + 1 : r + 17] - q)
+                - ON[kind, r - 1 : r + 15] * (q - B[l, r - 1 : r + 15])
             )
             PL[at] = biharmonic_mix * lap - lateral_mix * q
 

time: 35.8 us -> 34.4 us (0.961)
  Pallas kernels: 31.6 us -> 30.2 us
    pallas_call x1, Pallas kernels: 31.6 us -> 30.2 us  [per_device(): pl.pallas_call(functools.partial(kernel, lat_n, lon_n, levels, rows, bloc...]
where the time goes in v2:
time: 34.4 us; the launch traced here: 34.3 us
  Pallas kernels  30.2 us (88%)
  local copies, waits for them, and re-layouts  3.38 us (10%)
  between operations  0.65 us (2%)
    pallas_call x1, Pallas kernels, per_device(): pl.pallas_call(functools.partial(kernel, lat_n, lon_n, levels, rows, bloc...  30.2 us
    unnamed x4, local copies, waits for them, and re-layouts  3.38 us

profile of v2, /device:TPU:1, one launch (start us, length us, event | category | flops | bytes accessed | tf_op | source)
XLA Modules:
  0.0 34.3 jit_solution(9446107137559906978)
XLA Ops:
  0.6 30.2 %shard_map.86 = (f32[2,8,192,128]{3,2,1,0:T(8,128)}, f32[192,128]{1,0:T(8,128)}) custom-call(f32[2,8,192,128]{3,2,1,0:T(8,128)} %tr.1, f32[2,8,192,128]{3,2,1,0:T(8,128)} %vel.1, s32[192,128]{1,0:T(8,128)} %mask_in.1, f32[96,128]{1,0:T(8,128)} %atm.1, f32[12,4,16,16]{3,2,1,0:T(8,128)} %wt.1, s32[4,12]{1,0:T(4,128)} %bitcast.1, s32[12]{0:T(128)} %cnt.1), custom_call_target="tpu_custom_call" | custom-call | tf_op jit(solution)/shard_map/pallas_call | solution.py:498
  30.9 0.0 copy-start
  30.9 2.7 %copy.11 = f32[2,8,192,128]{3,2,1,0:T(8,128)} copy(f32[2,8,192,128]{3,2,1,0:T(8,128)} %get-tuple-element.4) | data formatting | bytes 3145728
  33.6 0.0 copy-done
  33.6 0.6 %copy.12 = f32[192,128]{1,0:T(8,128)} copy(f32[192,128]{1,0:T(8,128)S(1)} %copy-done) | data formatting | bytes 196608
Async XLA Ops:
  30.9 2.7 %copy-start = (f32[192,128]{1,0:T(8,128)S(1)}, f32[192,128]{1,0:T(8,128)}, u32[]{:S(2)}) copy-start(f32[192,128]{1,0:T(8,128)} %get-tuple-element.5) | copy-start | bytes 294916
